TPU v7x, 512 devices: a whole 4x4x16 slice. The times are simulated.
512 devices in a mesh: rows: 128 (over z, y, core), cols: 4 (over x).
Axes of the slice: x: 4, y: 4, z: 16, core: 2. Of those that a mesh axis runs over, the one named last changes fastest.
Arguments:
- latent: bfloat16 [4, 128, 1024], P(None, 'rows', 'cols'), may hold values from -18 to 18
- deep: bfloat16 [320, 128, 1024], P(None, 'rows', 'cols'), may hold values from -6 to 6
- timestep: int32 [1], replicated, may hold values from 0 to 999
- in_weight: bfloat16 [36, 320], replicated, may hold values from -1 to 1
- front_weight: bfloat16 [5760, 320], P('rows'), may hold values from -0.078125 to 0.078125
- middle_weight: bfloat16 [2880, 320], P('cols'), may hold values from -0.109375 to 0.109375
- skip_weight: bfloat16 [640, 320], P('cols'), may hold values from -0.25 to 0.25
- out_weight: bfloat16 [2880, 4], replicated, may hold values from -0.109375 to 0.109375
- time_weight: bfloat16 [320, 1280], replicated, may hold values from -0.3125 to 0.3125
- time_second: bfloat16 [1280, 1280], P('cols'), may hold values from -0.15625 to 0.15625
- time_proj: bfloat16 [1280, 320], replicated, may hold values from -0.15625 to 0.15625
- input_gain: float32 [640], replicated, may hold values from 0.1 to 1.9
- middle_gain: float32 [320], replicated, may hold values from 0.1 to 1.9
- output_gain: float32 [320], replicated, may hold values from 0.1 to 1.9
Outputs:
- noise: float32 [4, 128, 1024], P(None, 'rows', 'cols')
All inputs are finite; a program needn't handle non-finite values.
Results may differ from a plain program's by a relative error of at most 0.0047.
Values may be sent and summed in bfloat16 or wider, within the bound.
No kernel may reach another device: no remote copies, remote signals or barrier semaphores. Data moves between devices by JAX's collectives and lax.ppermute only.
A program may use at most 64 MiB of HBM per device.

v0:
```python
import math
import jax
import jax.numpy as jnp
from jax import lax
from jax.sharding import Mesh
from jax.sharding import PartitionSpec as P

GROUPS = 32
ROWS = ("rows_0", "rows_1", "rows_2")
epsilon = 1e-05


def from_everyone(x, axis):
    count = lax.axis_size(axis)
    return lax.all_to_all(jnp.broadcast_to(x[None], (count, *x.shape)), axis, 0, 0, tiled=True)


def taken_together(x, axis):
    return from_everyone(x, axis).sum(axis=0)


def over_axes(x, axes):
    far, near = axes
    nearer = taken_together(x, near)
    return taken_together(nearer, far)


def together(arrays, axis):
    vector, at, finished = (jnp.concatenate([a.reshape(-1) for a in arrays]), 0, [])
    subtotal = over_axes(vector, axis)
    for a in arrays:
        finished.append(subtotal[at : at + a.size].reshape(a.shape))
        at += a.size
    return tuple(finished)


def laid_out(parts, dim):
    shape = list(parts.shape[1:])
    shape[dim] *= parts.shape[0]
    return jnp.moveaxis(parts, 0, dim).reshape(shape)


def gather_directly(x, axis, dim):
    return laid_out(from_everyone(x, axis), dim)


def padded_2(cells, sides, width):
    for axis, dim in sides:
        count = lax.axis_size(axis)
        ends = count - 1
        head = lax.slice_in_dim(cells, 0, width, axis=dim)
        tail = lax.slice_in_dim(cells, cells.shape[dim] - width, cells.shape[dim], axis=dim)
        cells = jnp.concatenate(
            [
                lax.ppermute(tail, axis, [(i, (i + 1) % count) for i in range(ends)]),
                cells,
                lax.ppermute(head, axis, [((i + 1) % count, i) for i in range(ends)]),
            ],
            axis=dim,
        )
    return cells


def unfold(padded, row_count, col_count):
    shifted = [
        padded[:, row_step : row_step + row_count, col_step : col_step + col_count]
        for row_step in range(3)
        for col_step in range(3)
    ]
    return jnp.stack(shifted, 0).reshape(9 * padded.shape[0], row_count * col_count)


def project(weight, columns):
    return lax.dot_general(
        weight, columns, (((0,), (0,)), ((), ())), preferred_element_type=jnp.float32
    )


def norm_silu(values, gain, members):
    grouped = values.reshape(GROUPS, -1)
    totals, squares = together(
        (jnp.sum(grouped, axis=1), jnp.sum(grouped * grouped, axis=1)),
        (("rows_0", "rows_1"), ("rows_2", "cols")),
    )
    center = totals / members
    offsets = grouped - center[:, None]
    spread = squares / members - center * center
    scaled = (offsets * lax.rsqrt(spread + epsilon)[:, None]).reshape(values.shape) * gain[:, None]
    return jax.nn.silu(scaled).astype(jnp.bfloat16)


def time_shift_of(timestep, time_weight, time_second, time_proj):
    half_width = time_weight.shape[0] // 2
    ratios = jnp.exp(-math.log(10000.0) * jnp.arange(half_width, dtype=jnp.float32) / half_width)
    angles = timestep[0].astype(jnp.float32) * ratios
    features = jnp.concatenate([jnp.cos(angles), jnp.sin(angles)])
    hidden = jax.nn.silu(
        jnp.dot(features, time_weight.astype(jnp.float32), precision=lax.Precision.HIGHEST)
    )
    embedded = jnp.dot(hidden, time_second.astype(jnp.float32), precision=lax.Precision.HIGHEST)
    return jnp.dot(
        jax.nn.silu(embedded), time_proj.astype(jnp.float32), precision=lax.Precision.HIGHEST
    )


def shards(
    latent,
    deep,
    timestep,
    in_weight,
    front_weight,
    middle_weight,
    skip_weight,
    out_weight,
    time_weight,
    time_second,
    time_proj,
    input_gain,
    middle_gain,
    output_gain,
):
    rows_here = latent.shape[1]
    cols_here = latent.shape[2]
    pixels = rows_here * cols_here
    image_cells = pixels * lax.axis_size(ROWS) * lax.axis_size("cols")
    channels = deep.shape[0]
    full_middle, full_skip, full_second = (
        gather_directly(middle_weight, "cols", 0),
        gather_directly(skip_weight, "cols", 0),
        gather_directly(time_second, "cols", 0),
    )
    time_shift = time_shift_of(timestep, time_weight, full_second, time_proj)
    padded_latent = padded_2(latent, ((ROWS, 1), ("cols", 2)), 1)
    skip_feat = project(in_weight, unfold(padded_latent, rows_here, cols_here)).astype(jnp.bfloat16)
    joined = jnp.concatenate([deep.reshape(channels, pixels), skip_feat], axis=0)
    members_wide = float(joined.shape[0] // GROUPS * image_cells)
    act_one = norm_silu(joined.astype(jnp.float32), input_gain, members_wide)
    padded_one = padded_2(act_one.reshape(-1, rows_here, cols_here), ((ROWS, 1), ("cols", 2)), 1)
    columns_one = unfold(padded_one, rows_here, cols_here)
    out_channels = front_weight.shape[1]
    hidden_one = project(lax.all_gather(front_weight, ROWS, axis=0, tiled=True), columns_one)
    hidden_one = hidden_one + time_shift[:, None]
    members_narrow = float(out_channels // GROUPS * image_cells)
    act_two = norm_silu(hidden_one, middle_gain, members_narrow)
    padded_two = padded_2(act_two.reshape(-1, rows_here, cols_here), ((ROWS, 1), ("cols", 2)), 1)
    block_out = project(full_middle, unfold(padded_two, rows_here, cols_here)) + project(
        full_skip, joined
    )
    act_three = norm_silu(block_out, output_gain, members_narrow)
    padded_three = padded_2(
        act_three.reshape(-1, rows_here, cols_here), ((ROWS, 1), ("cols", 2)), 1
    )
    noise = project(out_weight, unfold(padded_three, rows_here, cols_here))
    return noise.reshape(out_weight.shape[1], rows_here, cols_here)


def solution(mesh):
    finer = Mesh(
        mesh.devices.reshape(16, 4, 2, mesh.shape["cols"]), ("rows_0", "rows_1", "rows_2", "cols")
    )
    in_specs = (
        P(None, ROWS, "cols"),
        P(None, ROWS, "cols"),
        P(),
        P(),
        P(ROWS, None),
        P("cols", None),
        P("cols", None),
        P(),
        P(),
        P("cols", None),
        P(),
        P(),
        P(),
        P(),
    )
    out_specs = P(None, ROWS, "cols")
    return jax.shard_map(
        shards, mesh=finer, in_specs=in_specs, out_specs=out_specs, check_vma=False
    )
```

profile of v0, /device:TPU:25, one launch (start us, length us, event | category | flops | bytes accessed | tf_op | source)
XLA Modules:
  0.0 324.5 jit_solution(3858233901648060752)
XLA Ops:
  7.3 3.8 %collective-permute-start = (bf16[4,1,256]{2,0,1:T(4,128)(2,1)}, bf16[4,1,256]{2,0,1:T(4,128)(2,1)S(1)}, u32[]{:S(2)}, u32[]{:S(2)}) collective-permute-start(bf16[4,1,256]{2,0,1:T(4,128)(2,1)} %param.14), channel_id=1, source_target_pairs={{0,4},{4,8},{8,12},{12,16},{16,20},{20,24},{24,28},{28,32},{32,36}... | collective-permute-start | bytes 6152 | tf_op jit(solution)/shard_map/ppermute | solution.py:55
  13.7 4.6 %collective-permute-done.1 = bf16[4,1,256]{2,0,1:T(4,128)(2,1)S(1)} collective-permute-done((bf16[4,1,256]{2,0,1:T(4,128)(2,1)}, bf16[4,1,256]{2,0,1:T(4,128)(2,1)S(1)}, u32[]{:S(2)}, u32[]{:S(2)}) %collective-permute-start.1) | collective-permute-done | bytes 2080 | tf_op jit(solution)/shard_map/ppermute | solution.py:57
  29.6 8.5 %all_to_all.51 = f32[8,1,64]{2,1,0:T(1,128)S(1)} all-to-all(f32[8,1,64]{2,1,0:T(1,128)S(1)} %broadcast_in_dim.18), channel_id=1, replica_groups=mesh['rows_0'=16,'rows_1'=4,'rows_2'=2,'cols'=4] {'rows_2','cols'}, dimensions={0} | all-to-all | bytes 4096 | tf_op jit(solution)/shard_map/all_to_all | solution.py:15
  38.7 17.7 %all-to-all-start.1 = ((f32[64,1,64]{2,1,0:T(1,128)}), f32[64,1,64]{2,1,0:T(1,128)S(1)}, u32[]{:S(2)}, u32[]{:S(2)}) async-start(f32[64,1,64]{2,1,0:T(1,128)} %broadcast_in_dim.19), calls=%async_computation.1 | async-start | bytes 65536 | tf_op jit(solution)/shard_map/all_to_all | solution.py:15
  57.1 11.1 %all-to-all-done.1 = f32[64,1,64]{2,1,0:T(1,128)S(1)} async-done(((f32[64,1,64]{2,1,0:T(1,128)}), f32[64,1,64]{2,1,0:T(1,128)S(1)}, u32[]{:S(2)}, u32[]{:S(2)}) %all-to-all-start.1) | async-done | bytes 16416 | tf_op jit(solution)/shard_map/all_to_all | solution.py:15
  70.2 4.8 %all-to-all-start.2 = ((bf16[4,320,1280]{2,1,0:T(8,128)(2,1)}), bf16[4,320,1280]{2,1,0:T(8,128)(2,1)}, u32[]{:S(2)}, u32[]{:S(2)}) async-start(bf16[4,320,1280]{2,1,0:T(8,128)(2,1)} %broadcast_in_dim.20), calls=%async_computation.2 | async-start | bytes 6553600 | tf_op jit(solution)/shard_map/all_to_all | solution.py:15
  75.8 6.3 %collective-permute-start.4 = (bf16[640,1,256]{2,0,1:T(8,128)(2,1)S(1)}, bf16[640,1,256]{2,0,1:T(8,128)(2,1)S(1)}, u32[]{:S(2)}, u32[]{:S(2)}) collective-permute-start(bf16[640,1,256]{2,0,1:T(8,128)(2,1)S(1)} %multiply_convert_fusion.1), channel_id=1, source_target_pairs={{0,4},{4,8},{8,12},{12,16},{16,20},{20,24},{24,28},{28,32},{32,36}... | collective-permute-start | bytes 983048 | tf_op jit(solution)/shard_map/ppermute | solution.py:55
  86.1 6.5 %collective-permute-done.5 = bf16[640,1,256]{2,0,1:T(8,128)(2,1)S(1)} collective-permute-done((bf16[640,1,256]{2,0,1:T(8,128)(2,1)S(1)}, bf16[640,1,256]{2,0,1:T(8,128)(2,1)S(1)}, u32[]{:S(2)}, u32[]{:S(2)}) %collective-permute-start.5) | collective-permute-done | bytes 327712 | tf_op jit(solution)/shard_map/ppermute | solution.py:57
  97.9 21.1 %collective-permute-done.6 = bf16[640,3,1]{2,0,1:T(8,128)(2,1)S(1)} collective-permute-done((bf16[640,3,1]{2,0,1:T(8,128)(2,1)S(1)}, bf16[640,3,1]{2,0,1:T(8,128)(2,1)S(1)}, u32[]{:S(2)}, u32[]{:S(2)}) %collective-permute-start.6) | collective-permute-done | bytes 3872 | tf_op jit(solution)/shard_map/ppermute | solution.py:55
  131.5 25.0 %all-gather.3.cloned.1.call-done = bf16[128,45,320]{2,1,0:T(8,128)(2,1)} async-done(((bf16[1,45,320]{2,1,0:T(8,128)(2,1)}), bf16[128,45,320]{2,1,0:T(8,128)(2,1)}) %all-gather.3.cloned.1.call-update) | async-done | bytes 3686416 | tf_op jit(solution)/shard_map/all_gather | solution.py:141
  156.5 7.6 %reshape.371 = bf16[5760,320]{1,0:T(8,128)(2,1)} reshape(bf16[128,45,320]{2,1,0:T(8,128)(2,1)} %all-gather.3.cloned.1.call-done) | data formatting | bytes 7372800
  164.2 5.7 %fusion.41 = (f32[320]{0:T(512)S(1)}, f32[320]{0:T(512)S(1)}, f32[256,320]{0,1:T(8,128)}) fusion(f32[320]{0:T(512)S(1)} %convolution_reduce_fusion.2, bf16[5760,256]{1,0:T(8,128)(2,1)} %bitcast.24, bf16[5760,320]{1,0:T(8,128)(2,1)} %reshape.371), kind=kOutput, calls=%fused_computation.131 | convolution fusion | flops 944045440 | bytes 6967040 | tf_op jit(solution)/shard_map/dot_general | solution.py:74
  170.4 8.9 %all_to_all.52 = f32[8,1,64]{2,1,0:T(1,128)S(1)} all-to-all(f32[8,1,64]{2,1,0:T(1,128)S(1)} %broadcast_in_dim.21), channel_id=1, replica_groups=mesh['rows_0'=16,'rows_1'=4,'rows_2'=2,'cols'=4] {'rows_2','cols'}, dimensions={0} | all-to-all | bytes 4096 | tf_op jit(solution)/shard_map/all_to_all | solution.py:15
  183.5 8.5 %all-to-all-done.6 = bf16[4,160,320]{2,1,0:T(8,128)(2,1)S(1)} async-done(((bf16[4,160,320]{2,1,0:T(8,128)(2,1)}), bf16[4,160,320]{2,1,0:T(8,128)(2,1)S(1)}, u32[]{:S(2)}, u32[]{:S(2)}) %all-to-all-start.6) | async-done | bytes 409632 | tf_op jit(solution)/shard_map/all_to_all | solution.py:15
  192.0 22.1 %all_to_all.53 = f32[64,1,64]{2,1,0:T(1,128)S(1)} all-to-all(f32[64,1,64]{2,1,0:T(1,128)S(1)} %broadcast_in_dim.22), channel_id=1, replica_groups=mesh['rows_0'=16,'rows_1'=4,'rows_2'=2,'cols'=4] {'rows_0','rows_1'}, dimensions={0} | all-to-all | bytes 32768 | tf_op jit(solution)/shard_map/all_to_all | solution.py:15
  221.0 7.2 %collective-permute-start.8 = (bf16[320,1,256]{2,0,1:T(8,128)(2,1)S(1)}, bf16[320,1,256]{2,0,1:T(8,128)(2,1)S(1)}, u32[]{:S(2)}, u32[]{:S(2)}) collective-permute-start(bf16[320,1,256]{2,0,1:T(8,128)(2,1)S(1)} %fusion.62), channel_id=1, source_target_pairs={{0,4},{4,8},{8,12},{12,16},{16,20},{20,24},{24,28},{28,32},{32,36}... | collective-permute-start | bytes 491528 | tf_op jit(solution)/shard_map/ppermute | solution.py:55
  230.5 6.5 %collective-permute-done.9 = bf16[320,1,256]{2,0,1:T(8,128)(2,1)S(1)} collective-permute-done((bf16[320,1,256]{2,0,1:T(8,128)(2,1)S(1)}, bf16[320,1,256]{2,0,1:T(8,128)(2,1)S(1)}, u32[]{:S(2)}, u32[]{:S(2)}) %collective-permute-start.9) | collective-permute-done | bytes 163872 | tf_op jit(solution)/shard_map/ppermute | solution.py:57
  237.9 4.3 %collective-permute-start.10 = (bf16[320,3,1]{2,0,1:T(8,128)(2,1)}, bf16[320,3,1]{2,0,1:T(8,128)(2,1)}, u32[]{:S(2)}, u32[]{:S(2)}) collective-permute-start(bf16[320,3,1]{2,0,1:T(8,128)(2,1)} %get-tuple-element.16), channel_id=1, source_target_pairs={{0,1},{1,2},{2,3},{4,5},{5,6},{6,7},{8,9},{9,10},{10,11},{12,13},{... | collective-permute-start | bytes 5768 | tf_op jit(solution)/shard_map/ppermute | solution.py:55
  247.0 3.8 %reshape.365 = bf16[2880,320]{0,1:T(8,128)(2,1)S(1)} reshape(bf16[4,720,320]{1,0,2:T(4,128)(2,1)} %copy.28) | data formatting | bytes 3686400 | tf_op jit(solution)/shard_map/reshape | solution.py:40
  253.3 6.1 %collective-permute-done.11 = bf16[320,3,1]{2,0,1:T(8,128)(2,1)S(1)} collective-permute-done((bf16[320,3,1]{2,0,1:T(8,128)(2,1)S(1)}, bf16[320,3,1]{2,0,1:T(8,128)(2,1)S(1)}, u32[]{:S(2)}, u32[]{:S(2)}) %collective-permute-start.11) | collective-permute-done | bytes 1952 | tf_op jit(solution)/shard_map/ppermute | solution.py:57
  263.5 9.1 %all_to_all.54 = f32[8,1,64]{2,1,0:T(1,128)S(1)} all-to-all(f32[8,1,64]{2,1,0:T(1,128)S(1)} %broadcast_in_dim.25), channel_id=1, replica_groups=mesh['rows_0'=16,'rows_1'=4,'rows_2'=2,'cols'=4] {'rows_2','cols'}, dimensions={0} | all-to-all | bytes 4096 | tf_op jit(solution)/shard_map/all_to_all | solution.py:15
  272.6 18.1 %all_to_all.55 = f32[64,1,64]{2,1,0:T(1,128)S(1)} all-to-all(f32[64,1,64]{2,1,0:T(1,128)S(1)} %broadcast_in_dim.26), channel_id=1, replica_groups=mesh['rows_0'=16,'rows_1'=4,'rows_2'=2,'cols'=4] {'rows_0','rows_1'}, dimensions={0} | all-to-all | bytes 32768 | tf_op jit(solution)/shard_map/all_to_all | solution.py:15
  291.4 6.0 %collective-permute-start.12 = (bf16[320,1,256]{2,0,1:T(8,128)(2,1)S(1)}, bf16[320,1,256]{2,0,1:T(8,128)(2,1)S(1)}, u32[]{:S(2)}, u32[]{:S(2)}) collective-permute-start(bf16[320,1,256]{2,0,1:T(8,128)(2,1)S(1)} %fusion.61), channel_id=1, source_target_pairs={{0,4},{4,8},{8,12},{12,16},{16,20},{20,24},{24,28},{28,32},{32,36}... | collective-permute-start | bytes 491528 | tf_op jit(solution)/shard_map/ppermute | solution.py:55
  299.7 6.5 %collective-permute-done.13 = bf16[320,1,256]{2,0,1:T(8,128)(2,1)S(1)} collective-permute-done((bf16[320,1,256]{2,0,1:T(8,128)(2,1)S(1)}, bf16[320,1,256]{2,0,1:T(8,128)(2,1)S(1)}, u32[]{:S(2)}, u32[]{:S(2)}) %collective-permute-start.13) | collective-permute-done | bytes 163872 | tf_op jit(solution)/shard_map/ppermute | solution.py:57
  (169 shorter events, 80.4 us)
Async XLA Ops:
  6.5 77.7 %copy-start = (bf16[320,1280]{1,0:T(8,128)(2,1)S(1)}, bf16[320,1280]{1,0:T(8,128)(2,1)}, u32[]{:S(2)}) copy-start(bf16[320,1280]{1,0:T(8,128)(2,1)} %param.22) | copy-start | bytes 2457604
  6.5 61.6 %copy-start.6 = (bf16[320,1280]{1,0:T(8,128)(2,1)S(1)}, bf16[320,1280]{1,0:T(8,128)(2,1)}, u32[]{:S(2)}) copy-start(bf16[320,1280]{1,0:T(8,128)(2,1)} %param.23) | copy-start | bytes 2457604
  6.5 150.0 %all-gather.3.cloned.1.call-start = ((), (), s32[]{:S(2)}) async-start(), calls=%async_computation.9 | async-start | bytes 4755456 | tf_op jit(solution)/shard_map/all_gather | solution.py:141
  7.3 5.7 %collective-permute-start = (bf16[4,1,256]{2,0,1:T(4,128)(2,1)}, bf16[4,1,256]{2,0,1:T(4,128)(2,1)S(1)}, u32[]{:S(2)}, u32[]{:S(2)}) collective-permute-start(bf16[4,1,256]{2,0,1:T(4,128)(2,1)} %param.14), channel_id=1, source_target_pairs={{0,4},{4,8},{8,12},{12,16},{16,20},{20,24},{24,28},{28,32},{32,36}... | collective-permute-start | bytes 6152 | tf_op jit(solution)/shard_map/ppermute | solution.py:55
  11.0 7.2 %collective-permute-start.1 = (bf16[4,1,256]{2,0,1:T(4,128)(2,1)}, bf16[4,1,256]{2,0,1:T(4,128)(2,1)S(1)}, u32[]{:S(2)}, u32[]{:S(2)}) collective-permute-start(bf16[4,1,256]{2,0,1:T(4,128)(2,1)} %param.14), channel_id=1, source_target_pairs={{4,0},{8,4},{12,8},{16,12},{20,16},{24,20},{28,24},{32,28},{36,32}... | collective-permute-start | bytes 6152 | tf_op jit(solution)/shard_map/ppermute | solution.py:57
  18.4 4.4 %collective-permute-start.2 = (bf16[4,3,1]{2,0,1:T(4,128)(2,1)S(1)}, bf16[4,3,1]{2,0,1:T(4,128)(2,1)S(1)}, u32[]{:S(2)}, u32[]{:S(2)}) collective-permute-start(bf16[4,3,1]{2,0,1:T(4,128)(2,1)S(1)} %get-tuple-element.18), channel_id=1, source_target_pairs={{0,1},{1,2},{2,3},{4,5},{5,6},{6,7},{8,9},{9,10},{10,11},{12,13},{... | collective-permute-start | bytes 80 | tf_op jit(solution)/shard_map/ppermute | solution.py:55
  21.5 4.3 %collective-permute-start.3 = (bf16[4,3,1]{2,0,1:T(4,128)(2,1)S(1)}, bf16[4,3,1]{2,0,1:T(4,128)(2,1)S(1)}, u32[]{:S(2)}, u32[]{:S(2)}) collective-permute-start(bf16[4,3,1]{2,0,1:T(4,128)(2,1)S(1)} %get-tuple-element.17), channel_id=1, source_target_pairs={{1,0},{2,1},{3,2},{5,4},{6,5},{7,6},{9,8},{10,9},{11,10},{13,12},{... | collective-permute-start | bytes 80 | tf_op jit(solution)/shard_map/ppermute | solution.py:57
  38.7 29.4 %all-to-all-start.1 = ((f32[64,1,64]{2,1,0:T(1,128)}), f32[64,1,64]{2,1,0:T(1,128)S(1)}, u32[]{:S(2)}, u32[]{:S(2)}) async-start(f32[64,1,64]{2,1,0:T(1,128)} %broadcast_in_dim.19), calls=%async_computation.1 | async-start | bytes 65536 | tf_op jit(solution)/shard_map/all_to_all | solution.py:15
  70.2 57.1 %all-to-all-start.2 = ((bf16[4,320,1280]{2,1,0:T(8,128)(2,1)}), bf16[4,320,1280]{2,1,0:T(8,128)(2,1)}, u32[]{:S(2)}, u32[]{:S(2)}) async-start(bf16[4,320,1280]{2,1,0:T(8,128)(2,1)} %broadcast_in_dim.20), calls=%async_computation.2 | async-start | bytes 6553600 | tf_op jit(solution)/shard_map/all_to_all | solution.py:15
  75.8 10.3 %collective-permute-start.4 = (bf16[640,1,256]{2,0,1:T(8,128)(2,1)S(1)}, bf16[640,1,256]{2,0,1:T(8,128)(2,1)S(1)}, u32[]{:S(2)}, u32[]{:S(2)}) collective-permute-start(bf16[640,1,256]{2,0,1:T(8,128)(2,1)S(1)} %multiply_convert_fusion.1), channel_id=1, source_target_pairs={{0,4},{4,8},{8,12},{12,16},{16,20},{20,24},{24,28},{28,32},{32,36}... | collective-permute-start | bytes 983048 | tf_op jit(solution)/shard_map/ppermute | solution.py:55
  82.1 10.5 %collective-permute-start.5 = (bf16[640,1,256]{2,0,1:T(8,128)(2,1)S(1)}, bf16[640,1,256]{2,0,1:T(8,128)(2,1)S(1)}, u32[]{:S(2)}, u32[]{:S(2)}) collective-permute-start(bf16[640,1,256]{2,0,1:T(8,128)(2,1)S(1)} %multiply_convert_fusion.1), channel_id=1, source_target_pairs={{4,0},{8,4},{12,8},{16,12},{20,16},{24,20},{28,24},{32,28},{36,32}... | collective-permute-start | bytes 983048 | tf_op jit(solution)/shard_map/ppermute | solution.py:57
  93.0 26.0 %collective-permute-start.6 = (bf16[640,3,1]{2,0,1:T(8,128)(2,1)S(1)}, bf16[640,3,1]{2,0,1:T(8,128)(2,1)S(1)}, u32[]{:S(2)}, u32[]{:S(2)}) collective-permute-start(bf16[640,3,1]{2,0,1:T(8,128)(2,1)S(1)} %get-tuple-element.12), channel_id=1, source_target_pairs={{0,1},{1,2},{2,3},{4,5},{5,6},{6,7},{8,9},{9,10},{10,11},{12,13},{... | collective-permute-start | bytes 11528 | tf_op jit(solution)/shard_map/ppermute | solution.py:55
  96.6 24.2 %collective-permute-start.7 = (bf16[640,3,1]{2,0,1:T(8,128)(2,1)S(1)}, bf16[640,3,1]{2,0,1:T(8,128)(2,1)S(1)}, u32[]{:S(2)}, u32[]{:S(2)}) collective-permute-start(bf16[640,3,1]{2,0,1:T(8,128)(2,1)S(1)} %get-tuple-element.11), channel_id=1, source_target_pairs={{1,0},{2,1},{3,2},{5,4},{6,5},{7,6},{9,8},{10,9},{11,10},{13,12},{... | collective-permute-start | bytes 11528 | tf_op jit(solution)/shard_map/ppermute | solution.py:57
  169.8 44.3 %copy-start.7 = (bf16[720,320]{0,1:T(8,128)(2,1)S(1)}, bf16[720,320]{0,1:T(8,128)(2,1)}, u32[]{:S(2)}) copy-start(bf16[720,320]{0,1:T(8,128)(2,1)} %param.19) | copy-start | bytes 1382404
  180.0 12.0 %all-to-all-start.6 = ((bf16[4,160,320]{2,1,0:T(8,128)(2,1)}), bf16[4,160,320]{2,1,0:T(8,128)(2,1)S(1)}, u32[]{:S(2)}, u32[]{:S(2)}) async-start(bf16[4,160,320]{2,1,0:T(8,128)(2,1)} %broadcast_in_dim.24), calls=%async_computation.6 | async-start | bytes 983040 | tf_op jit(solution)/shard_map/all_to_all | solution.py:15
  215.5 28.7 %all-to-all-start.5 = ((bf16[4,720,320]{1,2,0:T(8,128)(2,1)}), bf16[4,720,320]{1,2,0:T(8,128)(2,1)S(1)}, u32[]{:S(2)}, u32[]{:S(2)}) async-start(bf16[4,720,320]{1,2,0:T(8,128)(2,1)} %broadcast_in_dim.23), calls=%async_computation.5 | async-start | bytes 3932160 | tf_op jit(solution)/shard_map/all_to_all | solution.py:15
  221.0 9.4 %collective-permute-start.8 = (bf16[320,1,256]{2,0,1:T(8,128)(2,1)S(1)}, bf16[320,1,256]{2,0,1:T(8,128)(2,1)S(1)}, u32[]{:S(2)}, u32[]{:S(2)}) collective-permute-start(bf16[320,1,256]{2,0,1:T(8,128)(2,1)S(1)} %fusion.62), channel_id=1, source_target_pairs={{0,4},{4,8},{8,12},{12,16},{16,20},{20,24},{24,28},{28,32},{32,36}... | collective-permute-start | bytes 491528 | tf_op jit(solution)/shard_map/ppermute | solution.py:55
  228.2 8.7 %collective-permute-start.9 = (bf16[320,1,256]{2,0,1:T(8,128)(2,1)S(1)}, bf16[320,1,256]{2,0,1:T(8,128)(2,1)S(1)}, u32[]{:S(2)}, u32[]{:S(2)}) collective-permute-start(bf16[320,1,256]{2,0,1:T(8,128)(2,1)S(1)} %fusion.62), channel_id=1, source_target_pairs={{4,0},{8,4},{12,8},{16,12},{20,16},{24,20},{28,24},{32,28},{36,32}... | collective-permute-start | bytes 491528 | tf_op jit(solution)/shard_map/ppermute | solution.py:57
  237.9 14.3 %collective-permute-start.10 = (bf16[320,3,1]{2,0,1:T(8,128)(2,1)}, bf16[320,3,1]{2,0,1:T(8,128)(2,1)}, u32[]{:S(2)}, u32[]{:S(2)}) collective-permute-start(bf16[320,3,1]{2,0,1:T(8,128)(2,1)} %get-tuple-element.16), channel_id=1, source_target_pairs={{0,1},{1,2},{2,3},{4,5},{5,6},{6,7},{8,9},{9,10},{10,11},{12,13},{... | collective-permute-start | bytes 5768 | tf_op jit(solution)/shard_map/ppermute | solution.py:55
  250.8 8.6 %collective-permute-start.11 = (bf16[320,3,1]{2,0,1:T(8,128)(2,1)S(1)}, bf16[320,3,1]{2,0,1:T(8,128)(2,1)S(1)}, u32[]{:S(2)}, u32[]{:S(2)}) collective-permute-start(bf16[320,3,1]{2,0,1:T(8,128)(2,1)S(1)} %copy-done.9), channel_id=1, source_target_pairs={{1,0},{2,1},{3,2},{5,4},{6,5},{7,6},{9,8},{10,9},{11,10},{13,12},{... | collective-permute-start | bytes 5768 | tf_op jit(solution)/shard_map/ppermute | solution.py:57
  291.4 8.2 %collective-permute-start.12 = (bf16[320,1,256]{2,0,1:T(8,128)(2,1)S(1)}, bf16[320,1,256]{2,0,1:T(8,128)(2,1)S(1)}, u32[]{:S(2)}, u32[]{:S(2)}) collective-permute-start(bf16[320,1,256]{2,0,1:T(8,128)(2,1)S(1)} %fusion.61), channel_id=1, source_target_pairs={{0,4},{4,8},{8,12},{12,16},{16,20},{20,24},{24,28},{28,32},{32,36}... | collective-permute-start | bytes 491528 | tf_op jit(solution)/shard_map/ppermute | solution.py:55
  297.4 8.7 %collective-permute-start.13 = (bf16[320,1,256]{2,0,1:T(8,128)(2,1)S(1)}, bf16[320,1,256]{2,0,1:T(8,128)(2,1)S(1)}, u32[]{:S(2)}, u32[]{:S(2)}) collective-permute-start(bf16[320,1,256]{2,0,1:T(8,128)(2,1)S(1)} %fusion.61), channel_id=1, source_target_pairs={{4,0},{8,4},{12,8},{16,12},{20,16},{24,20},{28,24},{32,28},{36,32}... | collective-permute-start | bytes 491528 | tf_op jit(solution)/shard_map/ppermute | solution.py:57
  306.4 5.3 %collective-permute-start.14 = (bf16[320,3,1]{2,0,1:T(8,128)(2,1)S(1)}, bf16[320,3,1]{2,0,1:T(8,128)(2,1)S(1)}, u32[]{:S(2)}, u32[]{:S(2)}) collective-permute-start(bf16[320,3,1]{2,0,1:T(8,128)(2,1)S(1)} %get-tuple-element.14), channel_id=1, source_target_pairs={{0,1},{1,2},{2,3},{4,5},{5,6},{6,7},{8,9},{9,10},{10,11},{12,13},{... | collective-permute-start | bytes 5768 | tf_op jit(solution)/shard_map/ppermute | solution.py:55
  308.6 6.9 %collective-permute-start.15 = (bf16[320,3,1]{2,0,1:T(8,128)(2,1)S(1)}, bf16[320,3,1]{2,0,1:T(8,128)(2,1)S(1)}, u32[]{:S(2)}, u32[]{:S(2)}) collective-permute-start(bf16[320,3,1]{2,0,1:T(8,128)(2,1)S(1)} %get-tuple-element.13), channel_id=1, source_target_pairs={{1,0},{2,1},{3,2},{5,4},{6,5},{7,6},{9,8},{10,9},{11,10},{13,12},{... | collective-permute-start | bytes 5768 | tf_op jit(solution)/shard_map/ppermute | solution.py:57
  (12 other events, 124.0 us)
Sparse Core Ops, SparseCore 0:
  10.4 146.0 all-gather.2
where the time goes:
time: 326 us; the launch traced here: 325 us
  waiting for transfers between devices  107 us (33%)
  starting transfers between devices  79.1 us (24%)
  blocking collectives  66.7 us (20%)
  local copies, waits for them, and re-layouts  26.1 us (8%)
  other arithmetic  16.3 us (5%)
  between operations  14.7 us (5%)
  matrix products  14.4 us (4%)
    all_to_all x5, blocking collectives, from_everyone(): lax.all_to_all(jnp.broadcast_to(x[None], (count, *x.shape)), axis, 0, 0,...  66.7 us
    ppermute x8, waiting for transfers between devices, padded_2(): lax.ppermute(head, axis, [((i + 1) % count, i) for i in range(ends)])  37 us
    ppermute x8, starting transfers between devices, padded_2(): lax.ppermute(tail, axis, [(i, (i + 1) % count) for i in range(ends)])  36.5 us
    all_to_all x4, starting transfers between devices, from_everyone(): lax.all_to_all(jnp.broadcast_to(x[None], (count, *x.shape)), axis, 0, 0,...  29.7 us
    ppermute x8, waiting for transfers between devices, padded_2(): lax.ppermute(tail, axis, [(i, (i + 1) % count) for i in range(ends)])  25 us
    all_gather x1, waiting for transfers between devices, shards(): lax.all_gather(front_weight, ROWS, axis=0, tiled=True)  25 us
    all_to_all x4, waiting for transfers between devices, from_everyone(): lax.all_to_all(jnp.broadcast_to(x[None], (count, *x.shape)), axis, 0, 0,...  19.6 us
    ppermute x8, starting transfers between devices, padded_2(): lax.ppermute(head, axis, [((i + 1) % count, i) for i in range(ends)])  13 us
  transfers between devices with their start and end apart: 21, of which 16 were waited for; matrix products, arithmetic and copies ran while one was open for 10% of the time, Pallas kernels for 0%

commit v1 on v0

--- a/solution.py
+++ b/solution.py
@@ -8,6 +8,13 @@
 GROUPS = 32
 ROWS = ("rows_0", "rows_1", "rows_2")
 epsilon = 1e-05
+
+
+def gather_over(shard, mesh_axis, dim):
+    peers = lax.axis_size(mesh_axis)
+    blocks = jnp.stack([shard for _ in range(peers)])
+    blocks = lax.all_to_all(blocks, mesh_axis, split_axis=0, concat_axis=0)
+    return jnp.concatenate(blocks, axis=dim)
 
 
 def from_everyone(x, axis):
@@ -138,7 +145,7 @@
     padded_one = padded_2(act_one.reshape(-1, rows_here, cols_here), ((ROWS, 1), ("cols", 2)), 1)
     columns_one = unfold(padded_one, rows_here, cols_here)
     out_channels = front_weight.shape[1]
-    hidden_one = project(lax.all_gather(front_weight, ROWS, axis=0, tiled=True), columns_one)
+    hidden_one = project(gather_over(front_weight, ROWS, 0), columns_one)
     hidden_one = hidden_one + time_shift[:, None]
     members_narrow = float(out_channels // GROUPS * image_cells)
     act_two = norm_silu(hidden_one, middle_gain, members_narrow)

time: 326 us -> 508 us (1.56)
  waiting for transfers between devices: 107 us -> 249 us
  blocking collectives: 66.7 us -> 140 us
  starting transfers between devices: 79.1 us -> 64.3 us
  between operations: 14.7 us -> 1.38 us
  other arithmetic: 16.3 us -> 11.1 us
    ppermute x8, waiting for transfers between devices: 25 us -> 204 us  [padded_2(): lax.ppermute(tail, axis, [(i, (i + 1) % count) for i in range(ends)])]
    all_to_all x5 -> x7, blocking collectives: 66.7 us -> 140 us  [from_everyone(): lax.all_to_all(jnp.broadcast_to(x[None], (count, *x.shape)), axis, 0, 0,...]
    all_gather x1 -> x0, waiting for transfers between devices: 25 us -> none  [shards(): lax.all_gather(front_weight, ROWS, axis=0, tiled=True)]
    all_to_all x4 -> x2, starting transfers between devices: 29.7 us -> 7.2 us  [from_everyone(): lax.all_to_all(jnp.broadcast_to(x[None], (count, *x.shape)), axis, 0, 0,...]
    all_to_all x0 -> x1, starting transfers between devices: none -> 11.6 us  [gather_over(): blocks = lax.all_to_all(blocks, mesh_axis, split_axis=0, concat_axis=0)]
    all_to_all x4 -> x2, waiting for transfers between devices: 19.6 us -> 8.47 us  [from_everyone(): lax.all_to_all(jnp.broadcast_to(x[None], (count, *x.shape)), axis, 0, 0,...]
    reshape x0 -> x1, local copies, waits for them, and re-layouts: none -> 7.64 us  [gather_over(): return jnp.concatenate(blocks, axis=dim)]
    unnamed x42 -> x45, local copies, waits for them, and re-layouts: 11 us -> 4.45 us
  transfers between devices with their start and end apart: 21 -> 19, of which waited for: 16 -> 14; matrix products, arithmetic and copies ran while one was open for 10% -> 4% of each run, Pallas kernels for 0% -> 0%
where the time goes in v1:
time: 508 us; the launch traced here: 507 us
  waiting for transfers between devices  249 us (49%)
  blocking collectives  140 us (28%)
  starting transfers between devices  64.3 us (13%)
  local copies, waits for them, and re-layouts  28.6 us (6%)
  matrix products  12.4 us (2%)
  other arithmetic  11.1 us (2%)
    ppermute x8, waiting for transfers between devices, padded_2(): lax.ppermute(tail, axis, [(i, (i + 1) % count) for i in range(ends)])  204 us
    all_to_all x7, blocking collectives, from_everyone(): lax.all_to_all(jnp.broadcast_to(x[None], (count, *x.shape)), axis, 0, 0,...  140 us
    ppermute x8, waiting for transfers between devices, padded_2(): lax.ppermute(head, axis, [((i + 1) % count, i) for i in range(ends)])  36 us
    ppermute x8, starting transfers between devices, padded_2(): lax.ppermute(tail, axis, [(i, (i + 1) % count) for i in range(ends)])  32.1 us
    ppermute x8, starting transfers between devices, padded_2(): lax.ppermute(head, axis, [((i + 1) % count, i) for i in range(ends)])  13.4 us
    all_to_all x1, starting transfers between devices, gather_over(): blocks = lax.all_to_all(blocks, mesh_axis, split_axis=0, concat_axis=0)  11.6 us
  transfers between devices with their start and end apart: 19, of which 14 were waited for; matrix products, arithmetic and copies ran while one was open for 4% of the time, Pallas kernels for 0%

profile of v1, /device:TPU:25, one launch (start us, length us, event | category | flops | bytes accessed | tf_op | source)
XLA Modules:
  0.0 506.6 jit_solution(2787025349475000043)
XLA Ops:
  0.0 3.9 collective-permute-start
  6.5 4.6 collective-permute-done.1
  22.5 8.5 %all_to_all.56 = f32[8,1,64]{2,1,0:T(1,128)S(1)} all-to-all(f32[8,1,64]{2,1,0:T(1,128)S(1)} %broadcast_in_dim.18), channel_id=1, replica_groups=mesh['rows_0'=16,'rows_1'=4,'rows_2'=2,'cols'=4] {'rows_2','cols'}, dimensions={0} | all-to-all | bytes 4096 | tf_op jit(solution)/shard_map/all_to_all | solution.py:22
  31.0 29.2 %all_to_all.57 = f32[64,1,64]{2,1,0:T(1,128)S(1)} all-to-all(f32[64,1,64]{2,1,0:T(1,128)S(1)} %broadcast_in_dim.19), channel_id=1, replica_groups=mesh['rows_0'=16,'rows_1'=4,'rows_2'=2,'cols'=4] {'rows_0','rows_1'}, dimensions={0} | all-to-all | bytes 32768 | tf_op jit(solution)/shard_map/all_to_all | solution.py:22
  61.6 40.1 %all_to_all.58 = bf16[4,320,1280]{2,1,0:T(8,128)(2,1)} all-to-all(bf16[4,320,1280]{2,1,0:T(8,128)(2,1)S(1)} %broadcast_in_dim.20), channel_id=1, replica_groups=mesh['rows_0'=16,'rows_1'=4,'rows_2'=2,'cols'=4] {'cols'}, dimensions={0} | all-to-all | bytes 6553600 | tf_op jit(solution)/shard_map/all_to_all | solution.py:22
  104.3 11.6 %all-to-all-start.2 = ((bf16[128,45,320]{2,1,0:T(8,128)(2,1)}), bf16[128,45,320]{2,1,0:T(8,128)(2,1)}, u32[]{:S(2)}, u32[]{:S(2)}) async-start(bf16[128,45,320]{2,1,0:T(8,128)(2,1)} %stack.95), calls=%async_computation.2 | async-start | bytes 9437184 | tf_op jit(solution)/shard_map/all_to_all | solution.py:16
  123.3 197.5 %collective-permute-done.4 = bf16[640,1,256]{2,0,1:T(8,128)(2,1)S(1)} collective-permute-done((bf16[640,1,256]{2,0,1:T(8,128)(2,1)S(1)}, bf16[640,1,256]{2,0,1:T(8,128)(2,1)S(1)}, u32[]{:S(2)}, u32[]{:S(2)}) %collective-permute-start.4) | collective-permute-done | bytes 327712 | tf_op jit(solution)/shard_map/ppermute | solution.py:62
  327.3 4.2 collective-permute-done.6
  341.5 7.6 %reshape.367 = bf16[5760,320]{1,0:T(8,128)(2,1)} reshape(bf16[128,45,320]{2,1,0:T(8,128)(2,1)} %all-to-all-done.2) | data formatting | bytes 7372800 | tf_op jit(solution)/shard_map/reshape | solution.py:17
  349.2 5.7 %fusion.41 = (f32[320]{0:T(512)S(1)}, f32[320]{0:T(512)S(1)}, f32[256,320]{0,1:T(8,128)}) fusion(f32[320]{0:T(512)S(1)} %convolution_reduce_fusion.2, bf16[5760,256]{1,0:T(8,128)(2,1)} %bitcast.211, bf16[5760,320]{1,0:T(8,128)(2,1)} %reshape.367), kind=kOutput, calls=%fused_computation.131 | convolution fusion | flops 944045440 | bytes 6967040 | tf_op jit(solution)/shard_map/dot_general | solution.py:81
  355.4 7.8 %all_to_all.59 = f32[8,1,64]{2,1,0:T(1,128)S(1)} all-to-all(f32[8,1,64]{2,1,0:T(1,128)S(1)} %broadcast_in_dim.21), channel_id=1, replica_groups=mesh['rows_0'=16,'rows_1'=4,'rows_2'=2,'cols'=4] {'rows_2','cols'}, dimensions={0} | all-to-all | bytes 4096 | tf_op jit(solution)/shard_map/all_to_all | solution.py:22
  367.5 8.5 %all-to-all-done.7 = bf16[4,160,320]{2,1,0:T(8,128)(2,1)S(1)} async-done(((bf16[4,160,320]{2,1,0:T(8,128)(2,1)}), bf16[4,160,320]{2,1,0:T(8,128)(2,1)S(1)}, u32[]{:S(2)}, u32[]{:S(2)}) %all-to-all-start.7) | async-done | bytes 409632 | tf_op jit(solution)/shard_map/all_to_all | solution.py:22
  376.0 27.0 %all_to_all.60 = f32[64,1,64]{2,1,0:T(1,128)S(1)} all-to-all(f32[64,1,64]{2,1,0:T(1,128)S(1)} %broadcast_in_dim.22), channel_id=1, replica_groups=mesh['rows_0'=16,'rows_1'=4,'rows_2'=2,'cols'=4] {'rows_0','rows_1'}, dimensions={0} | all-to-all | bytes 32768 | tf_op jit(solution)/shard_map/all_to_all | solution.py:22
  404.4 3.7 all-to-all-start.6
  409.9 7.0 %collective-permute-start.8 = (bf16[320,1,256]{2,0,1:T(8,128)(2,1)S(1)}, bf16[320,1,256]{2,0,1:T(8,128)(2,1)S(1)}, u32[]{:S(2)}, u32[]{:S(2)}) collective-permute-start(bf16[320,1,256]{2,0,1:T(8,128)(2,1)S(1)} %fusion.62), channel_id=1, source_target_pairs={{0,4},{4,8},{8,12},{12,16},{16,20},{20,24},{24,28},{28,32},{32,36}... | collective-permute-start | bytes 491528 | tf_op jit(solution)/shard_map/ppermute | solution.py:62
  419.1 6.5 %collective-permute-done.9 = bf16[320,1,256]{2,0,1:T(8,128)(2,1)S(1)} collective-permute-done((bf16[320,1,256]{2,0,1:T(8,128)(2,1)S(1)}, bf16[320,1,256]{2,0,1:T(8,128)(2,1)S(1)}, u32[]{:S(2)}, u32[]{:S(2)}) %collective-permute-start.9) | collective-permute-done | bytes 163872 | tf_op jit(solution)/shard_map/ppermute | solution.py:64
  426.6 4.3 collective-permute-start.10
  435.7 3.8 reshape.371
  442.2 5.7 %collective-permute-done.11 = bf16[320,3,1]{2,0,1:T(8,128)(2,1)S(1)} collective-permute-done((bf16[320,3,1]{2,0,1:T(8,128)(2,1)S(1)}, bf16[320,3,1]{2,0,1:T(8,128)(2,1)S(1)}, u32[]{:S(2)}, u32[]{:S(2)}) %collective-permute-start.11) | collective-permute-done | bytes 1952 | tf_op jit(solution)/shard_map/ppermute | solution.py:64
  451.9 9.6 %all_to_all.61 = f32[8,1,64]{2,1,0:T(1,128)S(1)} all-to-all(f32[8,1,64]{2,1,0:T(1,128)S(1)} %broadcast_in_dim.25), channel_id=1, replica_groups=mesh['rows_0'=16,'rows_1'=4,'rows_2'=2,'cols'=4] {'rows_2','cols'}, dimensions={0} | all-to-all | bytes 4096 | tf_op jit(solution)/shard_map/all_to_all | solution.py:22
  461.5 18.0 %all_to_all.62 = f32[64,1,64]{2,1,0:T(1,128)S(1)} all-to-all(f32[64,1,64]{2,1,0:T(1,128)S(1)} %broadcast_in_dim.26), channel_id=1, replica_groups=mesh['rows_0'=16,'rows_1'=4,'rows_2'=2,'cols'=4] {'rows_0','rows_1'}, dimensions={0} | all-to-all | bytes 32768 | tf_op jit(solution)/shard_map/all_to_all | solution.py:22
  480.3 6.0 %collective-permute-start.12 = (bf16[320,1,256]{2,0,1:T(8,128)(2,1)S(1)}, bf16[320,1,256]{2,0,1:T(8,128)(2,1)S(1)}, u32[]{:S(2)}, u32[]{:S(2)}) collective-permute-start(bf16[320,1,256]{2,0,1:T(8,128)(2,1)S(1)} %fusion.61), channel_id=1, source_target_pairs={{0,4},{4,8},{8,12},{12,16},{16,20},{20,24},{24,28},{28,32},{32,36}... | collective-permute-start | bytes 491528 | tf_op jit(solution)/shard_map/ppermute | solution.py:62
  488.5 6.5 %collective-permute-done.13 = bf16[320,1,256]{2,0,1:T(8,128)(2,1)S(1)} collective-permute-done((bf16[320,1,256]{2,0,1:T(8,128)(2,1)S(1)}, bf16[320,1,256]{2,0,1:T(8,128)(2,1)S(1)}, u32[]{:S(2)}, u32[]{:S(2)}) %collective-permute-start.13) | collective-permute-done | bytes 163872 | tf_op jit(solution)/shard_map/ppermute | solution.py:64
  500.7 3.7 collective-permute-done.15
  (171 shorter events, 74.3 us)
Async XLA Ops:
  0.0 122.8 %copy-start = (bf16[320,1280]{1,0:T(8,128)(2,1)S(1)}, bf16[320,1280]{1,0:T(8,128)(2,1)}, u32[]{:S(2)}) copy-start(bf16[320,1280]{1,0:T(8,128)(2,1)} %param.22) | copy-start | bytes 2457604
  0.0 5.8 %collective-permute-start = (bf16[4,1,256]{2,0,1:T(4,128)(2,1)}, bf16[4,1,256]{2,0,1:T(4,128)(2,1)S(1)}, u32[]{:S(2)}, u32[]{:S(2)}) collective-permute-start(bf16[4,1,256]{2,0,1:T(4,128)(2,1)} %param.14), channel_id=1, source_target_pairs={{0,4},{4,8},{8,12},{12,16},{16,20},{20,24},{24,28},{28,32},{32,36}... | collective-permute-start | bytes 6152 | tf_op jit(solution)/shard_map/ppermute | solution.py:62
  3.9 7.2 %collective-permute-start.1 = (bf16[4,1,256]{2,0,1:T(4,128)(2,1)}, bf16[4,1,256]{2,0,1:T(4,128)(2,1)S(1)}, u32[]{:S(2)}, u32[]{:S(2)}) collective-permute-start(bf16[4,1,256]{2,0,1:T(4,128)(2,1)} %param.14), channel_id=1, source_target_pairs={{4,0},{8,4},{12,8},{16,12},{20,16},{24,20},{28,24},{32,28},{36,32}... | collective-permute-start | bytes 6152 | tf_op jit(solution)/shard_map/ppermute | solution.py:64
  11.2 4.4 collective-permute-start.2
  14.3 4.3 collective-permute-start.3
  61.6 40.1 %copy-start.11 = (bf16[45,320]{1,0:T(8,128)(2,1)S(1)}, bf16[45,320]{1,0:T(8,128)(2,1)}, u32[]{:S(2)}) copy-start(bf16[45,320]{1,0:T(8,128)(2,1)} %param.18) | copy-start | bytes 86404
  104.3 237.3 %all-to-all-start.2 = ((bf16[128,45,320]{2,1,0:T(8,128)(2,1)}), bf16[128,45,320]{2,1,0:T(8,128)(2,1)}, u32[]{:S(2)}, u32[]{:S(2)}) async-start(bf16[128,45,320]{2,1,0:T(8,128)(2,1)} %stack.95), calls=%async_computation.2 | async-start | bytes 9437184 | tf_op jit(solution)/shard_map/all_to_all | solution.py:16
  117.4 203.3 %collective-permute-start.4 = (bf16[640,1,256]{2,0,1:T(8,128)(2,1)S(1)}, bf16[640,1,256]{2,0,1:T(8,128)(2,1)S(1)}, u32[]{:S(2)}, u32[]{:S(2)}) collective-permute-start(bf16[640,1,256]{2,0,1:T(8,128)(2,1)S(1)} %multiply_convert_fusion.1), channel_id=1, source_target_pairs={{0,4},{4,8},{8,12},{12,16},{16,20},{20,24},{24,28},{28,32},{32,36}... | collective-permute-start | bytes 983048 | tf_op jit(solution)/shard_map/ppermute | solution.py:62
  120.8 202.4 %collective-permute-start.5 = (bf16[640,1,256]{2,0,1:T(8,128)(2,1)S(1)}, bf16[640,1,256]{2,0,1:T(8,128)(2,1)S(1)}, u32[]{:S(2)}, u32[]{:S(2)}) collective-permute-start(bf16[640,1,256]{2,0,1:T(8,128)(2,1)S(1)} %multiply_convert_fusion.1), channel_id=1, source_target_pairs={{4,0},{8,4},{12,8},{16,12},{20,16},{24,20},{28,24},{32,28},{36,32}... | collective-permute-start | bytes 983048 | tf_op jit(solution)/shard_map/ppermute | solution.py:64
  323.5 8.0 %collective-permute-start.6 = (bf16[640,3,1]{2,0,1:T(8,128)(2,1)S(1)}, bf16[640,3,1]{2,0,1:T(8,128)(2,1)S(1)}, u32[]{:S(2)}, u32[]{:S(2)}) collective-permute-start(bf16[640,3,1]{2,0,1:T(8,128)(2,1)S(1)} %get-tuple-element.12), channel_id=1, source_target_pairs={{0,1},{1,2},{2,3},{4,5},{5,6},{6,7},{8,9},{9,10},{10,11},{12,13},{... | collective-permute-start | bytes 11528 | tf_op jit(solution)/shard_map/ppermute | solution.py:62
  325.8 9.6 %collective-permute-start.7 = (bf16[640,3,1]{2,0,1:T(8,128)(2,1)S(1)}, bf16[640,3,1]{2,0,1:T(8,128)(2,1)S(1)}, u32[]{:S(2)}, u32[]{:S(2)}) collective-permute-start(bf16[640,3,1]{2,0,1:T(8,128)(2,1)S(1)} %get-tuple-element.11), channel_id=1, source_target_pairs={{1,0},{2,1},{3,2},{5,4},{6,5},{7,6},{9,8},{10,9},{11,10},{13,12},{... | collective-permute-start | bytes 11528 | tf_op jit(solution)/shard_map/ppermute | solution.py:64
  354.8 48.1 %copy-start.7 = (bf16[720,320]{0,1:T(8,128)(2,1)S(1)}, bf16[720,320]{0,1:T(8,128)(2,1)}, u32[]{:S(2)}) copy-start(bf16[720,320]{0,1:T(8,128)(2,1)} %param.19) | copy-start | bytes 1382404
  364.0 12.0 %all-to-all-start.7 = ((bf16[4,160,320]{2,1,0:T(8,128)(2,1)}), bf16[4,160,320]{2,1,0:T(8,128)(2,1)S(1)}, u32[]{:S(2)}, u32[]{:S(2)}) async-start(bf16[4,160,320]{2,1,0:T(8,128)(2,1)} %broadcast_in_dim.24), calls=%async_computation.7 | async-start | bytes 983040 | tf_op jit(solution)/shard_map/all_to_all | solution.py:22
  375.9 28.4 %copy-start.3 = (bf16[4,160,320]{2,1,0:T(8,128)(2,1)}, bf16[4,160,320]{2,1,0:T(8,128)(2,1)S(1)}, u32[]{:S(2)}) copy-start(bf16[4,160,320]{2,1,0:T(8,128)(2,1)S(1)} %all-to-all-done.7) | copy-start | bytes 1228804
  404.4 28.5 %all-to-all-start.6 = ((bf16[4,720,320]{1,2,0:T(8,128)(2,1)}), bf16[4,720,320]{1,2,0:T(8,128)(2,1)S(1)}, u32[]{:S(2)}, u32[]{:S(2)}) async-start(bf16[4,720,320]{1,2,0:T(8,128)(2,1)} %broadcast_in_dim.23), calls=%async_computation.6 | async-start | bytes 3932160 | tf_op jit(solution)/shard_map/all_to_all | solution.py:22
  409.9 9.2 %collective-permute-start.8 = (bf16[320,1,256]{2,0,1:T(8,128)(2,1)S(1)}, bf16[320,1,256]{2,0,1:T(8,128)(2,1)S(1)}, u32[]{:S(2)}, u32[]{:S(2)}) collective-permute-start(bf16[320,1,256]{2,0,1:T(8,128)(2,1)S(1)} %fusion.62), channel_id=1, source_target_pairs={{0,4},{4,8},{8,12},{12,16},{16,20},{20,24},{24,28},{28,32},{32,36}... | collective-permute-start | bytes 491528 | tf_op jit(solution)/shard_map/ppermute | solution.py:62
  416.9 8.7 %collective-permute-start.9 = (bf16[320,1,256]{2,0,1:T(8,128)(2,1)S(1)}, bf16[320,1,256]{2,0,1:T(8,128)(2,1)S(1)}, u32[]{:S(2)}, u32[]{:S(2)}) collective-permute-start(bf16[320,1,256]{2,0,1:T(8,128)(2,1)S(1)} %fusion.62), channel_id=1, source_target_pairs={{4,0},{8,4},{12,8},{16,12},{20,16},{24,20},{28,24},{32,28},{36,32}... | collective-permute-start | bytes 491528 | tf_op jit(solution)/shard_map/ppermute | solution.py:64
  426.6 14.6 %collective-permute-start.10 = (bf16[320,3,1]{2,0,1:T(8,128)(2,1)}, bf16[320,3,1]{2,0,1:T(8,128)(2,1)}, u32[]{:S(2)}, u32[]{:S(2)}) collective-permute-start(bf16[320,3,1]{2,0,1:T(8,128)(2,1)} %get-tuple-element.16), channel_id=1, source_target_pairs={{0,1},{1,2},{2,3},{4,5},{5,6},{6,7},{8,9},{9,10},{10,11},{12,13},{... | collective-permute-start | bytes 5768 | tf_op jit(solution)/shard_map/ppermute | solution.py:62
  439.5 8.4 %collective-permute-start.11 = (bf16[320,3,1]{2,0,1:T(8,128)(2,1)S(1)}, bf16[320,3,1]{2,0,1:T(8,128)(2,1)S(1)}, u32[]{:S(2)}, u32[]{:S(2)}) collective-permute-start(bf16[320,3,1]{2,0,1:T(8,128)(2,1)S(1)} %copy-done.9), channel_id=1, source_target_pairs={{1,0},{2,1},{3,2},{5,4},{6,5},{7,6},{9,8},{10,9},{11,10},{13,12},{... | collective-permute-start | bytes 5768 | tf_op jit(solution)/shard_map/ppermute | solution.py:64
  450.6 29.5 %copy-start.16 = (f32[320]{0:T(512)S(1)}, f32[320]{0:T(512)}, u32[]{:S(2)}) copy-start(f32[320]{0:T(512)} %param.27) | copy-start | bytes 3844
  480.3 8.2 %collective-permute-start.12 = (bf16[320,1,256]{2,0,1:T(8,128)(2,1)S(1)}, bf16[320,1,256]{2,0,1:T(8,128)(2,1)S(1)}, u32[]{:S(2)}, u32[]{:S(2)}) collective-permute-start(bf16[320,1,256]{2,0,1:T(8,128)(2,1)S(1)} %fusion.61), channel_id=1, source_target_pairs={{0,4},{4,8},{8,12},{12,16},{16,20},{20,24},{24,28},{28,32},{32,36}... | collective-permute-start | bytes 491528 | tf_op jit(solution)/shard_map/ppermute | solution.py:62
  486.3 8.7 %collective-permute-start.13 = (bf16[320,1,256]{2,0,1:T(8,128)(2,1)S(1)}, bf16[320,1,256]{2,0,1:T(8,128)(2,1)S(1)}, u32[]{:S(2)}, u32[]{:S(2)}) collective-permute-start(bf16[320,1,256]{2,0,1:T(8,128)(2,1)S(1)} %fusion.61), channel_id=1, source_target_pairs={{4,0},{8,4},{12,8},{16,12},{20,16},{24,20},{28,24},{32,28},{36,32}... | collective-permute-start | bytes 491528 | tf_op jit(solution)/shard_map/ppermute | solution.py:64
  495.2 5.3 %collective-permute-start.14 = (bf16[320,3,1]{2,0,1:T(8,128)(2,1)S(1)}, bf16[320,3,1]{2,0,1:T(8,128)(2,1)S(1)}, u32[]{:S(2)}, u32[]{:S(2)}) collective-permute-start(bf16[320,3,1]{2,0,1:T(8,128)(2,1)S(1)} %get-tuple-element.14), channel_id=1, source_target_pairs={{0,1},{1,2},{2,3},{4,5},{5,6},{6,7},{8,9},{9,10},{10,11},{12,13},{... | collective-permute-start | bytes 5768 | tf_op jit(solution)/shard_map/ppermute | solution.py:62
  497.5 6.9 %collective-permute-start.15 = (bf16[320,3,1]{2,0,1:T(8,128)(2,1)S(1)}, bf16[320,3,1]{2,0,1:T(8,128)(2,1)S(1)}, u32[]{:S(2)}, u32[]{:S(2)}) collective-permute-start(bf16[320,3,1]{2,0,1:T(8,128)(2,1)S(1)} %get-tuple-element.13), channel_id=1, source_target_pairs={{1,0},{2,1},{3,2},{5,4},{6,5},{7,6},{9,8},{10,9},{11,10},{13,12},{... | collective-permute-start | bytes 5768 | tf_op jit(solution)/shard_map/ppermute | solution.py:64
  (12 other events, 89.9 us)
